TPU v7x, 32 devices: a whole 2x2x4 slice. The times are simulated.
32 devices in a mesh: grp: 2 (over x), st: 16 (over z, y, core).
Axes of the slice: x: 2, y: 2, z: 4, core: 2. Of those that a mesh axis runs over, the one named last changes fastest.
Arguments:
- ensemble: bfloat16 [128, 32768], P('st', 'grp'), parts along dimension 1, may hold values from -6 to 6
- obs_value: float32 [8, 4096], P('grp'), parts along dimension 0, may hold values from -6 to 6
- obs_spread: float32 [8, 4096], P('grp'), parts along dimension 0, may hold values from 0.5 to 2
- obs_noise: bfloat16 [8, 128, 4096], P('grp'), parts along dimension 0, may hold values from -5 to 5
- owner: int32 [8], P('grp'), parts along dimension 0, may hold values from 0 to 15, as said below
- obs_local: int32 [8, 4096], P('grp'), parts along dimension 0, may hold values from 0 to 1023, as said below
- loc_count: int32 [4, 128], P(None, ('grp', 'st')), parts along dimension 1, may hold values from 1 to 4, as said below
- loc_obs: int32 [4, 128, 4], P(None, ('grp', 'st')), parts along dimension 1, may hold values from 0 to 15
- loc_shift: int32 [4, 128, 4], P(None, ('grp', 'st')), parts along dimension 1, may hold values from 0 to 255
Outputs:
- analysis: bfloat16 [128, 32768], P(None, ('grp', 'st')), parts along dimension 1
There are 2 independent parts, one for each index of `grp`. A program takes and returns all parts, laid end to end along the dimension named above; each array names one. Nothing has to cross between parts.
Inputs may be any that keep to these rules, and one draw needn't show every extreme that they name: owner[b] is drawn uniformly over the regions. `obs_local`: observation block k of a batch observes variables k * (64) .. (k + 1) * 64 - 1 of the region. loc_count[b, i] slots of loc_obs and loc_shift are used for state block i; the others are ignored. Every state block has at least 1; the first state block of the observed region has 4. Regions are busy or quiet as a whole.
All inputs are finite; a program needn't handle non-finite values.
Results may differ from a plain program's by a relative error of at most 0.009.
Values may be sent and summed in bfloat16 or wider, within the bound.
A program may use at most 128 MiB of HBM per device.

v0:
```python
import math

import jax
import jax.numpy as jnp
from jax import lax
from jax.sharding import PartitionSpec as P

M = 128
BLK = 256
NB = 4
KMAX = 4


inflation = 4.0


def broadcast(value, axis, source):
    kept = jnp.where(lax.axis_index(axis) == source, value, 0).astype(value.dtype)
    return lax.psum(kept, axis)


def gains(rows, value, spread, noise):
    scale = math.sqrt(inflation) * spread
    center = jnp.mean(rows, axis=0, keepdims=True)
    norm_rows = (rows - center) / (scale * math.sqrt(M - 1.0))
    misfit = (value + scale * noise.astype(jnp.float32) - rows) / scale
    count = rows.shape[1] // BLK
    s_blocks = norm_rows.reshape(M, count, BLK).transpose(1, 0, 2)
    d_blocks = misfit.reshape(M, count, BLK).transpose(1, 0, 2)
    system = jnp.eye(M, dtype=jnp.float32)[None] + jnp.einsum(
        "kmo,kno->kmn", s_blocks, s_blocks, precision=lax.Precision.HIGHEST
    )
    right = jnp.einsum("kmo,kno->kmn", s_blocks, d_blocks, precision=lax.Precision.HIGHEST)
    lower = jnp.linalg.cholesky(system)
    inner = jax.scipy.linalg.solve_triangular(lower, right, lower=True)
    solved = jax.scipy.linalg.solve_triangular(lower, inner, lower=True, trans=1)
    return (solved / math.sqrt(M - 1.0)).astype(jnp.bfloat16)


def taper_of(shift):
    offsets = jnp.arange(BLK, dtype=jnp.float32)[None, :] - shift.astype(jnp.float32)[:, None]
    ratio = offsets / (BLK / 4.0)
    return 1.0 / (1.0 + ratio * ratio)


def shards(
    ensemble, obs_value, obs_spread, obs_noise, owner, obs_local, loc_count, loc_obs, loc_shift
):
    local = lax.all_to_all(ensemble, "st", split_axis=1, concat_axis=0, tiled=True)
    state = local.astype(jnp.float32)
    width = state.shape[1]
    blocks = width // BLK
    for batch in range(NB):
        rows = jnp.take(state, obs_local[batch], axis=1)
        rows = broadcast(rows.astype(jnp.bfloat16), "st", owner[batch]).astype(rows.dtype)
        weights = gains(rows, obs_value[batch], obs_spread[batch], obs_noise[batch])
        center = jnp.mean(state, axis=0, keepdims=True)
        anomalies = (state - center).astype(jnp.bfloat16).reshape(M, blocks, BLK)
        counts = loc_count[batch]
        pairs = loc_obs[batch]
        shifts = loc_shift[batch]
        zeros = jnp.zeros((M, blocks, BLK), jnp.float32)
        total = zeros
        for slot in range(KMAX):
            idx = lax.dynamic_index_in_dim(pairs, slot, 1, keepdims=False)
            shf = lax.dynamic_index_in_dim(shifts, slot, 1, keepdims=False)
            picked = jnp.take(weights, idx, axis=0)
            term = jnp.einsum("ilm,liv->miv", picked, anomalies, preferred_element_type=jnp.float32)
            factor = jnp.where((counts > slot)[:, None], taper_of(shf), 0.0)
            total = total + term * factor[None]
        state = state + total.reshape(M, width)
    return state.astype(jnp.bfloat16)


def solution(mesh):
    placed = (
        P("st", "grp"),
        P("grp", None),
        P("grp", None),
        P("grp", None, None),
        P("grp"),
        P("grp", None),
        P(None, ("grp", "st")),
        P(None, ("grp", "st"), None),
        P(None, ("grp", "st"), None),
    )
    return jax.shard_map(
        shards, mesh=mesh, in_specs=placed, out_specs=P(None, ("grp", "st")), check_vma=False
    )
```

profile of v0, /device:TPU:14, one launch (start us, length us, event | category | flops | bytes accessed | tf_op | source)
XLA Modules:
  0.0 2014.4 jit_solution(4573195112236070268)
XLA Ops:
  6.5 6.2 all-to-all-start
  14.0 1.3 slice_reduce_fusion
  23.2 1.5 fusion.157
  24.6 1.7 slice_multiply_fusion.1
  26.4 4.0 fusion.154
  50.1 11.0 gather_fusion
  61.1 2.9 fusion.60
  65.0 92.7 %all-reduce.5.cloned.1.call-done = bf16[128,4096]{0,1:T(8,128)(2,1)} async-done(((bf16[128,4096]{0,1:T(8,128)(2,1)}), bf16[128,4096]{0,1:T(8,128)(2,1)}) %all-reduce.5.cloned.1.call-update) | async-done | bytes 1048592 | tf_op jit(solution)/shard_map/psum | solution.py:19
  157.8 1.6 convert_reduce_fusion.3
  159.3 6.9 fusion
  166.3 1.8 copy.103
  168.1 1.9 copy.98
  170.0 4.6 fusion.27
  174.7 3.2 fusion.32
  177.8 1.6 copy.100
  180.6 188.4 %custom-call.18 = f32[16,128,128]{2,1,0:T(8,128)S(1)} custom-call(f32[16,128,128]{2,1,0:T(8,128)} %fusion.79), custom_call_target="Cholesky" | custom-call | tf_op jit(solution)/shard_map/jit(cholesky)/cholesky | solution.py:34
  370.5 158.2 %custom-call.20 = f32[16,1,128,128]{2,3,1,0:T(8,128)S(1)} custom-call(f32[16,1,128,128]{3,2,1,0:T(8,128)} %select_bitcast_fusion.3), custom_call_target="InvertDiagBlocksLowerTriangular" | custom-call | tf_op jit(solution)/shard_map/jit(_solve_triangular)/vmap()/triangular_solve | solution.py:36
  528.7 1.9 fusion.76
  537.5 13.0 gather_fusion.5
  550.5 2.9 fusion.61
  554.1 2.7 copy.146
  557.5 1.3 copy.147
  559.6 86.5 %all-reduce.7.cloned.1.call-done = bf16[128,4096]{0,1:T(8,128)(2,1)} async-done(((bf16[128,4096]{0,1:T(8,128)(2,1)}), bf16[128,4096]{0,1:T(8,128)(2,1)}) %all-reduce.7.cloned.1.call-update) | async-done | bytes 1048592 | tf_op jit(solution)/shard_map/psum | solution.py:19
  646.1 1.6 convert_reduce_fusion.2
  647.8 6.2 fusion.2
  654.0 1.8 copy.116
  655.8 1.9 copy.111
  657.7 3.1 fusion.35
  660.9 3.1 fusion.22
  664.0 1.6 copy.113
  666.7 188.4 %custom-call.21 = f32[16,128,128]{2,1,0:T(8,128)S(1)} custom-call(f32[16,128,128]{2,1,0:T(8,128)} %fusion.75), custom_call_target="Cholesky" | custom-call | tf_op jit(solution)/shard_map/jit(cholesky)/cholesky | solution.py:34
  856.5 158.1 %custom-call.23 = f32[16,1,128,128]{2,3,1,0:T(8,128)S(1)} custom-call(f32[16,1,128,128]{3,2,1,0:T(8,128)} %select_bitcast_fusion.2), custom_call_target="InvertDiagBlocksLowerTriangular" | custom-call | tf_op jit(solution)/shard_map/jit(_solve_triangular)/vmap()/triangular_solve | solution.py:36
  1014.6 1.9 fusion.72
  1019.1 1.3 gather_fusion.8
  1020.4 1.5 gather_fusion.9
  1026.1 13.0 gather_fusion.10
  1039.2 2.9 fusion.62
  1042.8 91.9 %all-reduce.9.cloned.1.call-done = bf16[128,4096]{0,1:T(8,128)(2,1)} async-done(((bf16[128,4096]{0,1:T(8,128)(2,1)}), bf16[128,4096]{0,1:T(8,128)(2,1)}) %all-reduce.9.cloned.1.call-update) | async-done | bytes 1048592 | tf_op jit(solution)/shard_map/psum | solution.py:19
  1134.6 1.6 convert_reduce_fusion.1
  1136.3 6.5 fusion.4
  1142.8 2.9 copy.123
  1145.7 2.9 copy.118
  1148.7 4.5 fusion.38
  1153.2 4.7 fusion.17
  1157.8 1.3 copy.120
  1159.2 2.3 fusion.71
  1161.5 189.1 %custom-call.24 = f32[16,128,128]{2,1,0:T(8,128)} custom-call(f32[16,128,128]{2,1,0:T(8,128)} %fusion.71), custom_call_target="Cholesky" | custom-call | tf_op jit(solution)/shard_map/jit(cholesky)/cholesky | solution.py:34
  1352.0 2.4 select_bitcast_fusion.1
  1354.5 159.0 %custom-call.26 = f32[16,1,128,128]{2,3,1,0:T(8,128)} custom-call(f32[16,1,128,128]{3,2,1,0:T(8,128)} %select_bitcast_fusion.1), custom_call_target="InvertDiagBlocksLowerTriangular" | custom-call | tf_op jit(solution)/shard_map/jit(_solve_triangular)/vmap()/triangular_solve | solution.py:36
  1513.5 3.2 fusion.68
  1523.3 11.0 gather_fusion.15
  1534.3 2.9 fusion.63
  1537.9 2.3 copy.148
  1540.4 89.6 %all-reduce.11.cloned.1.call-done = bf16[128,4096]{0,1:T(8,128)(2,1)} async-done(((bf16[128,4096]{0,1:T(8,128)(2,1)}), bf16[128,4096]{0,1:T(8,128)(2,1)}) %all-reduce.11.cloned.1.call-update) | async-done | bytes 1048592 | tf_op jit(solution)/shard_map/psum | solution.py:19
  1630.0 1.6 convert_reduce_fusion
  1631.6 6.9 fusion.6
  1638.4 1.8 copy.130
  1640.3 2.1 copy.125
  1642.4 3.2 fusion.41
  1645.5 3.1 fusion.12
  1648.6 1.6 copy.127
  1651.4 188.4 %custom-call.27 = f32[16,128,128]{2,1,0:T(8,128)S(1)} custom-call(f32[16,128,128]{2,1,0:T(8,128)} %fusion.67), custom_call_target="Cholesky" | custom-call | tf_op jit(solution)/shard_map/jit(cholesky)/cholesky | solution.py:34
  1841.3 158.2 %custom-call.29 = f32[16,1,128,128]{2,3,1,0:T(8,128)S(1)} custom-call(f32[16,1,128,128]{3,2,1,0:T(8,128)} %select_bitcast_fusion), custom_call_target="InvertDiagBlocksLowerTriangular" | custom-call | tf_op jit(solution)/shard_map/jit(_solve_triangular)/vmap()/triangular_solve | solution.py:36
  1999.4 1.9 fusion.64
  (251 shorter events, 66.0 us)
Async XLA Ops:
  6.5 43.3 %all-to-all-start = ((bf16[8,16,1024]{2,0,1:T(8,128)(2,1)}), bf16[8,16,1024]{2,0,1:T(8,128)(2,1)S(1)}, u32[]{:S(2)}, u32[]{:S(2)}) async-start(bf16[8,16,1024]{2,0,1:T(8,128)(2,1)} %bitcast.255), calls=%async_computation | async-start | bytes 524288 | tf_op jit(solution)/shard_map/all_to_all | solution.py:49
  12.8 145.0 %all-reduce.5.cloned.1.call-start = ((), (), s32[]{:S(2)}) async-start(), calls=%async_computation.1 | async-start | bytes 2097152 | tf_op jit(solution)/shard_map/psum | solution.py:19
  26.4 4.0 copy-start.25
  64.1 582.1 %all-reduce.7.cloned.1.call-start = ((), (), s32[]{:S(2)}) async-start(), calls=%async_computation.2 | async-start | bytes 2097152 | tf_op jit(solution)/shard_map/psum | solution.py:19
  64.9 494.5 %copy-start.6 = (f32[128,4,256]{0,2,1:T(8,128)}, f32[128,4,256]{0,2,1:T(8,128)S(1)}, u32[]{:S(2)}) copy-start(f32[128,4,256]{0,2,1:T(8,128)S(1)} %copy.110) | copy-start | bytes 1572868
  177.8 1.7 copy-start.3
  180.6 348.0 %copy-start.11 = (f32[16,128,128]{2,1,0:T(8,128)S(1)}, f32[16,128,128]{2,1,0:T(8,128)}, u32[]{:S(2)}) copy-start(f32[16,128,128]{2,1,0:T(8,128)} %fusion.27) | copy-start | bytes 3145732
  530.5 4.1 copy-start.40
  530.5 4.1 copy-start.54
  531.8 4.2 copy-start.39
  531.8 4.2 copy-start.53
  533.9 2.4 copy-start.38
  533.9 2.4 copy-start.52
  537.4 22.0 %copy-start.4 = (f32[4,256,128]{2,1,0:T(8,128)}, f32[4,256,128]{2,1,0:T(8,128)S(1)}, u32[]{:S(2)}) copy-start(f32[4,256,128]{2,1,0:T(8,128)S(1)} %get-tuple-element.95) | copy-start | bytes 1572868
  537.5 13.0 copy-start.28
  550.5 3.0 copy-start.57
  553.4 4.0 copy-start.16
  553.4 581.2 %all-reduce.9.cloned.1.call-start = ((), (), s32[]{:S(2)}) async-start(), calls=%async_computation.3 | async-start | bytes 2097152 | tf_op jit(solution)/shard_map/psum | solution.py:19
  554.1 5.3 copy-start.41
  557.4 90.3 %copy-start.21 = (f32[1,4096]{1,0:T(1,128)S(1)}, f32[1,4096]{1,0:T(1,128)}, u32[]{:S(2)}) copy-start(f32[1,4096]{1,0:T(1,128)} %get-tuple-element.60) | copy-start | bytes 49156
  557.5 90.3 %copy-start.22 = (f32[1,4096]{1,0:T(1,128)S(1)}, f32[1,4096]{1,0:T(1,128)}, u32[]{:S(2)}) copy-start(f32[1,4096]{1,0:T(1,128)} %get-tuple-element.63) | copy-start | bytes 49156
  557.5 90.3 %copy-start.24 = (f32[1,4096]{1,0:T(1,128)S(1)}, f32[1,4096]{1,0:T(1,128)}, u32[]{:S(2)}) copy-start(f32[1,4096]{1,0:T(1,128)} %get-tuple-element.67) | copy-start | bytes 49156
  657.7 3.1 copy-start.9
  664.0 1.7 copy-start.2
  666.7 347.9 %copy-start.12 = (f32[16,128,128]{2,1,0:T(8,128)S(1)}, f32[16,128,128]{2,1,0:T(8,128)}, u32[]{:S(2)}) copy-start(f32[16,128,128]{2,1,0:T(8,128)} %fusion.22) | copy-start | bytes 3145732
  1020.4 4.5 copy-start.5
  1020.4 4.5 copy-start.7
  1021.9 2.0 copy-start.18
  1021.9 3.0 copy-start.17
  1021.9 3.1 copy-start.37
  1021.9 3.1 copy-start.51
  1026.1 13.0 copy-start.27
  1039.1 3.0 copy-start.56
  1039.1 3.6 copy-start.42
  1039.1 97.1 %copy-start.19 = (f32[1,4096]{1,0:T(1,128)S(1)}, f32[1,4096]{1,0:T(1,128)}, u32[]{:S(2)}) copy-start(f32[1,4096]{1,0:T(1,128)} %get-tuple-element.61) | copy-start | bytes 49156
  1039.1 97.1 %copy-start.20 = (f32[1,4096]{1,0:T(1,128)S(1)}, f32[1,4096]{1,0:T(1,128)}, u32[]{:S(2)}) copy-start(f32[1,4096]{1,0:T(1,128)} %get-tuple-element.65) | copy-start | bytes 49156
  1039.1 97.1 %copy-start.23 = (f32[1,4096]{1,0:T(1,128)S(1)}, f32[1,4096]{1,0:T(1,128)}, u32[]{:S(2)}) copy-start(f32[1,4096]{1,0:T(1,128)} %get-tuple-element.69) | copy-start | bytes 49156
  1042.1 94.2 %copy-start.14 = (bf16[1,128,4096]{1,2,0:T(8,128)(2,1)S(1)}, bf16[1,128,4096]{1,2,0:T(8,128)(2,1)}, u32[]{:S(2)}) copy-start(bf16[1,128,4096]{1,2,0:T(8,128)(2,1)} %copy.147) | copy-start | bytes 3145732
  1042.1 587.9 %all-reduce.11.cloned.1.call-start = ((), (), s32[]{:S(2)}) async-start(), calls=%async_computation.4 | async-start | bytes 2097152 | tf_op jit(solution)/shard_map/psum | solution.py:19
  1148.7 4.5 copy-start
  1161.5 352.0 %copy-start.13 = (f32[16,128,128]{2,1,0:T(8,128)S(1)}, f32[16,128,128]{2,1,0:T(8,128)}, u32[]{:S(2)}) copy-start(f32[16,128,128]{2,1,0:T(8,128)} %fusion.17) | copy-start | bytes 3145732
  1513.5 3.2 copy-start.15
  1516.7 4.1 copy-start.36
  1516.7 4.1 copy-start.50
  1516.7 4.5 copy-start.34
  1516.7 4.5 copy-start.44
  1518.0 3.8 copy-start.35
  1518.0 3.8 copy-start.45
  1520.8 1.6 copy-start.33
  1520.8 1.6 copy-start.43
  1523.3 11.0 copy-start.26
  1534.3 2.9 copy-start.55
  1642.4 3.2 copy-start.8
  1648.6 1.7 copy-start.1
  1651.4 348.0 %copy-start.10 = (f32[16,128,128]{2,1,0:T(8,128)S(1)}, f32[16,128,128]{2,1,0:T(8,128)}, u32[]{:S(2)}) copy-start(f32[16,128,128]{2,1,0:T(8,128)} %fusion.12) | copy-start | bytes 3145732
  2001.3 4.1 copy-start.32
  2001.3 4.1 copy-start.49
  2001.3 4.4 copy-start.30
  2001.3 4.4 copy-start.47
  2002.5 3.5 copy-start.31
  2002.6 3.5 copy-start.48
  2004.7 1.7 copy-start.29
  2004.7 1.7 copy-start.46
Sparse Core Ops, SparseCore 0:
  64.2 93.5 all-reduce.4
  553.6 92.5 all-reduce.6
  1042.2 92.3 all-reduce.8
  1537.4 92.5 all-reduce.10
where the time goes:
time: 2020 us; the launch traced here: 2010 us
  other arithmetic  1470 us (73%)
  waiting for transfers between devices  361 us (18%)
  local copies, waits for them, and re-layouts  102 us (5%)
  matrix products  53.3 us (3%)
    another operation x13, other arithmetic, gains(): lower = jnp.linalg.cholesky(system)  756 us
    another operation x9, other arithmetic, gains(): jax.scipy.linalg.solve_triangular(lower, inner, lower=True, trans=1)  640 us
    psum x4, waiting for transfers between devices, broadcast(): return lax.psum(kept, axis)  361 us
    gather x4, local copies, waits for them, and re-layouts, shards(): rows = jnp.take(state, obs_local[batch], axis=1)  48 us
  transfers between devices with their start and end apart: 5, of which 4 were waited for; matrix products, arithmetic and copies ran while one was open for 2% of the time, Pallas kernels for 0%

commit v1 on v0

v1 whole, which is shorter than its diff:
```python
import functools
import math

import jax
import jax.numpy as jnp
from jax import lax
from jax.experimental import pallas as pl
from jax.experimental.pallas import tpu as pltpu
from jax.sharding import PartitionSpec as P

M = 128
BLK = 256
NB = 4
KMAX = 4
SPAN = 64
PAIR = 2 * SPAN
REGION = 1024
BLOCKS = REGION // BLK
NOB = REGION // SPAN
ENTRY = 1 + 2 * KMAX
TABLE = NB * BLOCKS * ENTRY
ROOT = math.sqrt(M - 1.0)
inflation = 4.0
HIGHEST = lax.Precision.HIGHEST
NT = (((1,), (1,)), ((), ()))


def prepare(value_ref, spread_ref, local_ref, noise_ref, rhs_ref, weight_ref):
    def one(k, carry):
        cols = pl.ds(pl.multiple_of(k * BLK, BLK), BLK)
        inv = 1.0 / (math.sqrt(inflation) * spread_ref[0, :, cols])
        var = lax.broadcasted_iota(jnp.int32, (SPAN, BLK), 0) + k * SPAN
        hit = var == local_ref[0, :, cols]
        placed = jnp.where(hit, inv, 0.0)
        high = placed.astype(jnp.bfloat16)
        low = (placed - high.astype(jnp.float32)).astype(jnp.bfloat16)
        noise = noise_ref[0, :, cols]
        summed = lax.dot_general(high, noise, NT, preferred_element_type=jnp.float32)
        summed += lax.dot_general(low, noise, NT, preferred_element_type=jnp.float32)
        square = placed * inv
        weight = jnp.sum(square, axis=1, keepdims=True)
        summed += jnp.sum(square * value_ref[0, :, cols], axis=1, keepdims=True)
        rows = pl.ds(pl.multiple_of(k * SPAN, SPAN), SPAN)
        rhs_ref[0, rows, :] = summed
        weight_ref[0, rows, :] = jnp.broadcast_to(weight, (SPAN, M))
        return carry

    lax.fori_loop(0, NOB, one, 0)


def assimilate(table_ref, owned_ref, mine_ref, rhs_ref, weight_ref, out_ref,
               state, taper, system, right, factor, weights, anoms):
    lane = lax.broadcasted_iota(jnp.int32, (SPAN, PAIR), 1)
    first = lane < SPAN
    chunks = REGION // 128

    def bring_owned(c, carry):
        at = pl.multiple_of(c * 128, 128)
        state[pl.ds(at, 128), :] = owned_ref[:, pl.ds(at, 128)].astype(jnp.float32).T
        return carry

    lax.fori_loop(0, NB * chunks, bring_owned, 0)

    def bring_mine(c, carry):
        at = pl.multiple_of(c * 128, 128)
        state[pl.ds(NB * REGION + at, 128), :] = mine_ref[:, pl.ds(at, 128)].astype(jnp.float32).T
        return carry

    lax.fori_loop(0, chunks, bring_mine, 0)

    offset = (lax.broadcasted_iota(jnp.int32, (2 * BLK, M), 0) - BLK).astype(jnp.float32)
    ratio = offset / (BLK / 4.0)
    taper[...] = 1.0 / (1.0 + ratio * ratio)

    for batch in range(NB):

        def build(p, carry):
            rows = pl.ds(pl.multiple_of(p * PAIR, PAIR), PAIR)
            x = state[pl.ds(pl.multiple_of(batch * REGION + p * PAIR, PAIR), PAIR), :]
            anom = x - jnp.mean(x, axis=1, keepdims=True)
            weight = weight_ref[batch, rows, :]
            live = weight > 0.0
            inverse = jnp.where(live, lax.rsqrt(jnp.where(live, weight, 1.0)), 0.0)
            scaled = anom * (weight * inverse * (1.0 / ROOT))
            factor[rows, :] = scaled
            right[rows, :] = (rhs_ref[batch, rows, :] - weight * x) * (inverse * (1.0 / ROOT))
            gram = lax.dot_general(scaled, scaled, NT, precision=HIGHEST, preferred_element_type=jnp.float32)
            row = lax.broadcasted_iota(jnp.int32, (SPAN, PAIR), 0)
            eye = jnp.where(row == jnp.where(first, lane, lane - SPAN), 1.0, 0.0)
            packed = jnp.where(first, gram[:SPAN], gram[SPAN:]) + eye
            system[pl.ds(pl.multiple_of(p * SPAN, SPAN), SPAN), :] = packed
            return carry

        lax.fori_loop(0, NOB // 2, build, 0)

        def eliminate(j, carry):
            pick = jnp.where(first, j, j + SPAN)
            hit = lane == pick
            for p in range(NOB // 2):
                full = system[p * SPAN:(p + 1) * SPAN, :]
                row = system[pl.ds(p * SPAN + j, 1), :]
                column = jnp.take_along_axis(full, pick, axis=1)
                rows8 = jnp.broadcast_to(row, (8, PAIR))
                pivot = jnp.take_along_axis(rows8, pick[:8], axis=1)
                inv = 1.0 / pivot
                scaled = jnp.where(hit[:8], inv, rows8 * inv)[:1]
                system[p * SPAN:(p + 1) * SPAN, :] = jnp.where(hit, 0.0, full) - column * scaled
                system[pl.ds(p * SPAN + j, 1), :] = scaled
            return carry

        lax.fori_loop(0, SPAN, eliminate, 0)

        def finish(p, carry):
            rows = pl.ds(pl.multiple_of(p * PAIR, PAIR), PAIR)
            packed = system[pl.ds(pl.multiple_of(p * SPAN, SPAN), SPAN), :]
            whole = jnp.concatenate([jnp.where(first, packed, 0.0), jnp.where(first, 0.0, packed)], axis=0)
            solved = jnp.dot(whole, right[rows, :], precision=HIGHEST, preferred_element_type=jnp.float32)
            left = factor[rows, :].T
            lanes = lax.broadcasted_iota(jnp.int32, (M, PAIR), 1) < SPAN
            for half, keep in enumerate((lanes, jnp.logical_not(lanes))):
                made = jnp.dot(jnp.where(keep, left, 0.0), solved, precision=HIGHEST, preferred_element_type=jnp.float32)
                weights[2 * p + half] = made.astype(jnp.bfloat16)
            return carry

        lax.fori_loop(0, NOB // 2, finish, 0)

        def update(index, carry):
            region = batch + 1 + index // BLOCKS
            block = index % BLOCKS
            base = ((region * NB + batch) * BLOCKS + block) * ENTRY
            rows = pl.ds(pl.multiple_of((batch + 1) * REGION + index * BLK, BLK), BLK)
            x = state[rows, :]
            anoms[...] = (x - jnp.mean(x, axis=1, keepdims=True)).astype(jnp.bfloat16)

            def slot(j, carry):
                k = table_ref[base + 1 + j]
                shift = table_ref[base + 1 + KMAX + j]
                term = jnp.dot(anoms[...], weights[k], preferred_element_type=jnp.float32)
                state[rows, :] += term * taper[pl.ds(BLK - shift, BLK), :]
                return carry

            lax.fori_loop(0, table_ref[base], slot, 0)
            return carry

        lax.fori_loop(0, (NB - batch) * BLOCKS, update, 0)

    def leave(c, carry):
        at = pl.multiple_of(c * 128, 128)
        out_ref[:, pl.ds(at, 128)] = state[pl.ds(NB * REGION + at, 128), :].T.astype(jnp.bfloat16)
        return carry

    lax.fori_loop(0, chunks, leave, 0)


def shards(
    ensemble, obs_value, obs_spread, obs_noise, owner, obs_local, loc_count, loc_obs, loc_shift
):
    members = ensemble.shape[0]
    mine = lax.all_to_all(ensemble, "st", split_axis=1, concat_axis=0, tiled=True)
    table = jnp.concatenate([loc_count[:, :, None], loc_obs, loc_shift], axis=2)
    pad = -(-TABLE // (members * 128)) * 128
    flat = jnp.pad(table.reshape(TABLE).astype(jnp.bfloat16), (0, members * pad - TABLE))
    parts = [lax.dynamic_slice_in_dim(ensemble, owner[b] * REGION, REGION, 1) for b in range(NB)]
    sent = jnp.concatenate(parts + [flat.reshape(members, pad)], axis=1)
    got = lax.all_gather(sent, "st", axis=0, tiled=True)
    owned = got[:, :NB * REGION]
    tables = got[:, NB * REGION:].reshape(-1, members * pad)[:, :TABLE]
    picked = [lax.dynamic_slice_in_dim(tables, owner[b], 1, 0).reshape(TABLE) for b in range(NB)]
    all_tables = jnp.concatenate(
        [jnp.concatenate(picked).astype(jnp.int32), table.reshape(TABLE)]
    )

    rhs, weight = pl.pallas_call(
        prepare,
        grid=(NB,),
        in_specs=[
            pl.BlockSpec((1, 1, NOB * BLK), lambda b: (b, 0, 0)),
            pl.BlockSpec((1, 1, NOB * BLK), lambda b: (b, 0, 0)),
            pl.BlockSpec((1, 1, NOB * BLK), lambda b: (b, 0, 0)),
            pl.BlockSpec((1, M, NOB * BLK), lambda b: (b, 0, 0)),
        ],
        out_specs=[pl.BlockSpec((1, REGION, M), lambda b: (b, 0, 0))] * 2,
        out_shape=[jax.ShapeDtypeStruct((NB, REGION, M), jnp.float32)] * 2,
        compiler_params=pltpu.CompilerParams(vmem_limit_bytes=16 << 20),
        cost_estimate=pl.CostEstimate(flops=1 << 29, bytes_accessed=8 << 20, transcendentals=0),
        name="prepare",
    )(obs_value[:, None], obs_spread[:, None], obs_local[:, None], obs_noise)

    vmem = pl.BlockSpec(memory_space=pltpu.VMEM)
    return pl.pallas_call(
        assimilate,
        in_specs=[pl.BlockSpec(memory_space=pltpu.SMEM)] + [vmem] * 4,
        out_specs=vmem,
        out_shape=jax.ShapeDtypeStruct((M, REGION), jnp.bfloat16),
        scratch_shapes=[
            pltpu.VMEM(((NB + 1) * REGION, M), jnp.float32),
            pltpu.VMEM((2 * BLK, M), jnp.float32),
            pltpu.VMEM((NOB // 2 * SPAN, PAIR), jnp.float32),
            pltpu.VMEM((REGION, M), jnp.float32),
            pltpu.VMEM((REGION, M), jnp.float32),
            pltpu.VMEM((NOB, M, M), jnp.bfloat16),
            pltpu.VMEM((BLK, M), jnp.bfloat16),
        ],
        compiler_params=pltpu.CompilerParams(vmem_limit_bytes=40 << 20),
        name="assimilate",
    )(all_tables, owned, mine, rhs, weight)


def solution(mesh):
    placed = (
        P("st", "grp"),
        P("grp", None),
        P("grp", None),
        P("grp", None, None),
        P("grp"),
        P("grp", None),
        P(None, ("grp", "st")),
        P(None, ("grp", "st"), None),
        P(None, ("grp", "st"), None),
    )
    return jax.shard_map(
        shards, mesh=mesh, in_specs=placed, out_specs=P(None, ("grp", "st")), check_vma=False
    )
```

time: 2020 us -> 284 us (0.14)
  other arithmetic: 1470 us -> 0.95 us
  waiting for transfers between devices: 361 us -> 8.94 us
  Pallas kernels: 0 us -> 226 us
  local copies, waits for them, and re-layouts: 102 us -> 15.8 us
  matrix products: 53.3 us -> 0 us
    another operation x22 -> x0, other arithmetic: 1400 us -> none  [the longest x13 756 us: gains(): lower = jnp.linalg.cholesky(system)]
    psum x4 -> x0, waiting for transfers between devices: 361 us -> none  [broadcast(): return lax.psum(kept, axis)]
    pallas_call x0 -> x2, Pallas kernels: none -> 226 us  [the longest x1 216 us: shards(): pl.pallas_call(assimilate, in_specs=[pl.BlockSpec(memory_space=pltpu.SMEM...]
    gather x20 -> x0, local copies, waits for them, and re-layouts: 60.5 us -> none  [the longest x4 48 us: shards(): rows = jnp.take(state, obs_local[batch], axis=1)]
    dot_general x24 -> x0, matrix products: 39.7 us -> none  [the longest x4 15.5 us: gains(): jnp.einsum('kmo,kno->kmn', s_blocks, d_blocks, precision=lax.Precision.HI...]
    div x16 -> x0, other arithmetic: 32.3 us -> none  [the longest x4 26.6 us: gains(): norm_rows = (rows - center) / (scale * math.sqrt(M - 1.0))]
  transfers between devices with their start and end apart: 5 -> 2, of which waited for: 4 -> 1; matrix products, arithmetic and copies ran while one was open for 2% -> 2% of each run, Pallas kernels for 0% -> 4%
where the time goes in v1:
time: 284 us; the launch traced here: 282 us
  Pallas kernels  226 us (80%)
  between operations  23.2 us (8%)
  local copies, waits for them, and re-layouts  15.8 us (6%)
  waiting for transfers between devices  8.94 us (3%)
  starting transfers between devices  6.25 us (2%)
    pallas_call x1, Pallas kernels, shards(): pl.pallas_call(assimilate, in_specs=[pl.BlockSpec(memory_space=pltpu.SMEM...  216 us
    pallas_call x1, Pallas kernels, shards(): pl.pallas_call(prepare, grid=(NB,), in_specs=[pl.BlockSpec((1, 1, NOB * B...  10.8 us
    all_gather x1, waiting for transfers between devices, shards(): got = lax.all_gather(sent, 'st', axis=0, tiled=True)  8.92 us
    unnamed x12, local copies, waits for them, and re-layouts  8.63 us
    all_to_all x1, starting transfers between devices, shards(): lax.all_to_all(ensemble, 'st', split_axis=1, concat_axis=0, tiled=True)  6.25 us
  transfers between devices with their start and end apart: 2, of which 1 were waited for; matrix products, arithmetic and copies ran while one was open for 2% of the time, Pallas kernels for 4%

profile of v1, /device:TPU:14, one launch (start us, length us, event | category | flops | bytes accessed | tf_op | source)
XLA Modules:
  0.0 281.5 jit_solution(17063499917601820736)
XLA Ops:
  6.5 0.0 all-gather.2.cloned.1.call-start
  6.5 1.5 fusion.4
  10.4 0.8 copy.10
  11.2 0.8 pad_add_fusion
  12.0 0.1 reshape.25
  12.2 0.7 dynamic-slice_dynamic-update-slice_fusion.3
  12.9 0.7 dynamic-slice_dynamic-update-slice_fusion.2
  13.6 0.7 dynamic-slice_dynamic-update-slice_fusion.1
  14.3 0.7 dynamic-slice_dynamic-update-slice_fusion
  15.0 0.0 copy-start.3
  15.0 0.6 copy-done.3
  15.7 0.0 all-gather.2.cloned.1.call-update
  15.7 6.3 %all-to-all-start = ((bf16[8,16,1024]{2,0,1:T(8,128)(2,1)}), bf16[8,16,1024]{2,0,1:T(8,128)(2,1)S(1)}, u32[]{:S(2)}, u32[]{:S(2)}) async-start(bf16[8,16,1024]{2,0,1:T(8,128)(2,1)} %bitcast.12), calls=%async_computation | async-start | bytes 524288 | tf_op jit(solution)/shard_map/all_to_all | solution.py:159
  26.8 0.9 broadcast_in_dim.13.value_ref
  27.7 0.9 broadcast_in_dim.14.spread_ref
  28.6 0.9 broadcast_in_dim.15.local_ref
  31.9 0.0 copy-start
  31.9 2.2 copy-done
  34.1 10.8 %prepare.1 = (f32[4,1024,128]{2,1,0:T(8,128)S(1)}, f32[4,1024,128]{2,1,0:T(8,128)S(1)}) custom-call(f32[4,1,4096]{2,1,0:T(1,128)S(1)} %broadcast_in_dim.13.value_ref, f32[4,1,4096]{2,1,0:T(1,128)S(1)} %broadcast_in_dim.14.spread_ref, s32[4,1,4096]{2,1,0:T(1,128)S(1)} %broadcast_in_dim.15.local_ref, bf16[4,128,4096]{2,1,0:T(8,128)(2,1)S(1)} %copy-done), custom_call_target="tpu_custom_call" | custom-call | flops 536870912 | bytes 8388608 | tf_op jit(solution)/shard_map/prepare/pallas_call | solution.py:173
  45.0 0.0 copy-start.1
  45.0 1.3 copy-done.1
  46.3 8.9 %all-gather.2.cloned.1.call-done = bf16[128,4224]{1,0:T(8,128)(2,1)} async-done(((bf16[8,4224]{1,0:T(8,128)(2,1)}), bf16[128,4224]{1,0:T(8,128)(2,1)}) %all-gather.2.cloned.1.call-update) | async-done | bytes 1081360 | tf_op jit(solution)/shard_map/all_gather | solution.py:165
  55.2 0.8 slice.32
  56.0 1.3 slice.34.owned_ref
  57.4 0.1 maximum_convert_fusion
  57.4 0.1 pad_add_fusion.1.table_ref
  57.5 0.0 all-to-all-done
  57.5 0.0 copy-start.2
  57.5 1.6 copy-done.2
  59.1 215.6 %assimilate.1 = bf16[128,1024]{1,0:T(8,128)(2,1)} custom-call(s32[720]{0:T(1024)S(1)} %pad_add_fusion.1.table_ref, bf16[128,4096]{1,0:T(8,128)(2,1)S(1)} %slice.34.owned_ref, bf16[128,1024]{1,0:T(8,128)(2,1)S(1)} %bitcast.11, f32[4,1024,128]{2,1,0:T(8,128)S(1)} %get-tuple-element.7.rhs_ref, f32[4,1024,128]{2,1,0:T(8,128)S(1)} %copy-done.2), custom_call_target="tpu_custom_call" | custom-call | tf_op jit(solution)/shard_map/assimilate/pallas_call | solution.py:190
  (5 shorter events, 0.1 us)
Async XLA Ops:
  6.5 48.7 %all-gather.2.cloned.1.call-start = ((), (), s32[]{:S(2)}) async-start(), calls=%async_computation.1 | async-start | bytes 1148928 | tf_op jit(solution)/shard_map/all_gather | solution.py:165
  15.0 0.6 copy-start.3
  15.7 41.8 %all-to-all-start = ((bf16[8,16,1024]{2,0,1:T(8,128)(2,1)}), bf16[8,16,1024]{2,0,1:T(8,128)(2,1)S(1)}, u32[]{:S(2)}, u32[]{:S(2)}) async-start(bf16[8,16,1024]{2,0,1:T(8,128)(2,1)} %bitcast.12), calls=%async_computation | async-start | bytes 524288 | tf_op jit(solution)/shard_map/all_to_all | solution.py:159
  31.9 2.2 copy-start
  45.0 1.3 copy-start.1
  57.5 1.6 copy-start.2
Sparse Core Ops, SparseCore 0:
  15.8 39.3 all-gather.1

commit v2 on v1

--- a/solution.py
+++ b/solution.py
@@ -59,14 +59,14 @@
         state[pl.ds(at, 128), :] = owned_ref[:, pl.ds(at, 128)].astype(jnp.float32).T
         return carry
 
-    lax.fori_loop(0, NB * chunks, bring_owned, 0)
+    lax.fori_loop(0, NB * chunks, bring_owned, 0, unroll=4)
 
     def bring_mine(c, carry):
         at = pl.multiple_of(c * 128, 128)
         state[pl.ds(NB * REGION + at, 128), :] = mine_ref[:, pl.ds(at, 128)].astype(jnp.float32).T
         return carry
 
-    lax.fori_loop(0, chunks, bring_mine, 0)
+    lax.fori_loop(0, chunks, bring_mine, 0, unroll=4)
 
     offset = (lax.broadcasted_iota(jnp.int32, (2 * BLK, M), 0) - BLK).astype(jnp.float32)
     ratio = offset / (BLK / 4.0)
@@ -91,21 +91,23 @@
             system[pl.ds(pl.multiple_of(p * SPAN, SPAN), SPAN), :] = packed
             return carry
 
-        lax.fori_loop(0, NOB // 2, build, 0)
+        lax.fori_loop(0, NOB // 2, build, 0, unroll=4)
 
         def eliminate(j, carry):
             pick = jnp.where(first, j, j + SPAN)
             hit = lane == pick
-            for p in range(NOB // 2):
-                full = system[p * SPAN:(p + 1) * SPAN, :]
-                row = system[pl.ds(p * SPAN + j, 1), :]
-                column = jnp.take_along_axis(full, pick, axis=1)
-                rows8 = jnp.broadcast_to(row, (8, PAIR))
-                pivot = jnp.take_along_axis(rows8, pick[:8], axis=1)
-                inv = 1.0 / pivot
-                scaled = jnp.where(hit[:8], inv, rows8 * inv)[:1]
-                system[p * SPAN:(p + 1) * SPAN, :] = jnp.where(hit, 0.0, full) - column * scaled
-                system[pl.ds(p * SPAN + j, 1), :] = scaled
+            pairs = range(NOB // 2)
+            fulls = [system[p * SPAN:(p + 1) * SPAN, :] for p in pairs]
+            rows = system[pl.ds(j, NOB // 2, stride=SPAN), :]
+            inv = 1.0 / jnp.take_along_axis(rows, pick[:NOB // 2], axis=1)
+            scaled = jnp.where(hit[:NOB // 2], inv, rows * inv)
+            columns = [jnp.take_along_axis(full, pick, axis=1) for full in fulls]
+            made = [
+                jnp.where(hit, 0.0, fulls[p]) - columns[p] * scaled[p:p + 1] for p in pairs
+            ]
+            for p in pairs:
+                system[p * SPAN:(p + 1) * SPAN, :] = made[p]
+            system[pl.ds(j, NOB // 2, stride=SPAN), :] = scaled
             return carry
 
         lax.fori_loop(0, SPAN, eliminate, 0)
@@ -122,7 +124,7 @@
                 weights[2 * p + half] = made.astype(jnp.bfloat16)
             return carry
 
-        lax.fori_loop(0, NOB // 2, finish, 0)
+        lax.fori_loop(0, NOB // 2, finish, 0, unroll=4)
 
         def update(index, carry):
             region = batch + 1 + index // BLOCKS
@@ -149,7 +151,7 @@
         out_ref[:, pl.ds(at, 128)] = state[pl.ds(NB * REGION + at, 128), :].T.astype(jnp.bfloat16)
         return carry
 
-    lax.fori_loop(0, chunks, leave, 0)
+    lax.fori_loop(0, chunks, leave, 0, unroll=4)
 
 
 def shards(

time: 284 us -> 142 us (0.50)
  the two profiles are of different devices: /device:TPU:14 before, /device:TPU:0 now
where the time goes in v2:
time: 142 us; the launch traced here: 141 us
  Pallas kernels  82.7 us (58%)
  between operations  23.2 us (16%)
  local copies, waits for them, and re-layouts  15.7 us (11%)
  waiting for transfers between devices  10.7 us (8%)
  starting transfers between devices  7.4 us (5%)
    pallas_call x1, Pallas kernels, shards(): pl.pallas_call(assimilate, in_specs=[pl.BlockSpec(memory_space=pltpu.SMEM...  71.9 us
    pallas_call x1, Pallas kernels, shards(): pl.pallas_call(prepare, grid=(NB,), in_specs=[pl.BlockSpec((1, 1, NOB * B...  10.8 us
    all_gather x1, waiting for transfers between devices, shards(): got = lax.all_gather(sent, 'st', axis=0, tiled=True)  10.7 us
    unnamed x12, local copies, waits for them, and re-layouts  8.62 us
    all_to_all x1, starting transfers between devices, shards(): lax.all_to_all(ensemble, 'st', split_axis=1, concat_axis=0, tiled=True)  7.4 us
  transfers between devices with their start and end apart: 2, of which 1 were waited for; matrix products, arithmetic and copies ran while one was open for 4% of the time, Pallas kernels for 8%

profile of v2, /device:TPU:0, one launch (start us, length us, event | category | flops | bytes accessed | tf_op | source)
XLA Modules:
  0.0 140.7 jit_solution(7950500055588659044)
XLA Ops:
  6.5 0.0 all-gather.2.cloned.1.call-start
  6.5 1.5 %fusion.4 = (s32[1]{0:T(128)}, s32[1]{0:T(128)}, s32[1]{0:T(128)}, s32[1]{0:T(128)}) fusion(s32[4]{0:T(128)} %param.13), kind=kLoop, calls=%fused_computation.16 | loop fusion | bytes 32 | tf_op jit(solution)/shard_map/slice | solution.py:165
  10.4 0.8 copy.10
  11.2 0.8 pad_add_fusion
  12.0 0.1 reshape.25
  12.2 0.7 dynamic-slice_dynamic-update-slice_fusion.3
  12.9 0.7 dynamic-slice_dynamic-update-slice_fusion.2
  13.6 0.7 dynamic-slice_dynamic-update-slice_fusion.1
  14.3 0.7 dynamic-slice_dynamic-update-slice_fusion
  15.0 0.0 copy-start.3
  15.0 0.6 copy-done.3
  15.7 0.0 all-gather.2.cloned.1.call-update
  15.7 7.4 %all-to-all-start = ((bf16[8,16,1024]{2,0,1:T(8,128)(2,1)}), bf16[8,16,1024]{2,0,1:T(8,128)(2,1)S(1)}, u32[]{:S(2)}, u32[]{:S(2)}) async-start(bf16[8,16,1024]{2,0,1:T(8,128)(2,1)} %bitcast.12), calls=%async_computation | async-start | bytes 524288 | tf_op jit(solution)/shard_map/all_to_all | solution.py:161
  28.0 0.9 broadcast_in_dim.13.value_ref
  28.9 0.9 broadcast_in_dim.14.spread_ref
  29.8 0.9 broadcast_in_dim.15.local_ref
  33.1 0.0 copy-start
  33.1 2.2 %copy-done = bf16[4,128,4096]{2,1,0:T(8,128)(2,1)S(1)} copy-done((bf16[4,128,4096]{2,1,0:T(8,128)(2,1)S(1)}, bf16[4,128,4096]{2,1,0:T(8,128)(2,1)}, u32[]{:S(2)}) %copy-start) | copy-done | bytes 4194328
  35.3 10.8 %prepare.1 = (f32[4,1024,128]{2,1,0:T(8,128)S(1)}, f32[4,1024,128]{2,1,0:T(8,128)S(1)}) custom-call(f32[4,1,4096]{2,1,0:T(1,128)S(1)} %broadcast_in_dim.13.value_ref, f32[4,1,4096]{2,1,0:T(1,128)S(1)} %broadcast_in_dim.14.spread_ref, s32[4,1,4096]{2,1,0:T(1,128)S(1)} %broadcast_in_dim.15.local_ref, bf16[4,128,4096]{2,1,0:T(8,128)(2,1)S(1)} %copy-done), custom_call_target="tpu_custom_call" | custom-call | flops 536870912 | bytes 8388608 | tf_op jit(solution)/shard_map/prepare/pallas_call | solution.py:175
  46.1 0.0 copy-start.1
  46.1 1.3 copy-done.1
  47.4 10.7 %all-gather.2.cloned.1.call-done = bf16[128,4224]{1,0:T(8,128)(2,1)} async-done(((bf16[8,4224]{1,0:T(8,128)(2,1)}), bf16[128,4224]{1,0:T(8,128)(2,1)}) %all-gather.2.cloned.1.call-update) | async-done | bytes 1081360 | tf_op jit(solution)/shard_map/all_gather | solution.py:167
  58.1 0.8 slice.32
  58.9 1.3 slice.34.owned_ref
  60.3 0.1 maximum_convert_fusion
  60.3 0.1 pad_add_fusion.1.table_ref
  60.4 0.0 all-to-all-done
  60.4 0.0 copy-start.2
  60.4 1.6 %copy-done.2 = f32[4,1024,128]{2,1,0:T(8,128)S(1)} copy-done((f32[4,1024,128]{2,1,0:T(8,128)S(1)}, f32[4,1024,128]{2,1,0:T(8,128)}, u32[]{:S(2)}) %copy-start.2) | copy-done | bytes 2097176
  62.0 71.9 %assimilate.1 = bf16[128,1024]{1,0:T(8,128)(2,1)} custom-call(s32[720]{0:T(1024)S(1)} %pad_add_fusion.1.table_ref, bf16[128,4096]{1,0:T(8,128)(2,1)S(1)} %slice.34.owned_ref, bf16[128,1024]{1,0:T(8,128)(2,1)S(1)} %bitcast.11, f32[4,1024,128]{2,1,0:T(8,128)S(1)} %get-tuple-element.7.rhs_ref, f32[4,1024,128]{2,1,0:T(8,128)S(1)} %copy-done.2), custom_call_target="tpu_custom_call" | custom-call | tf_op jit(solution)/shard_map/assimilate/pallas_call | solution.py:192
  (5 shorter events, 0.1 us)
Async XLA Ops:
  6.5 51.6 %all-gather.2.cloned.1.call-start = ((), (), s32[]{:S(2)}) async-start(), calls=%async_computation.1 | async-start | bytes 1148928 | tf_op jit(solution)/shard_map/all_gather | solution.py:167
  15.0 0.6 copy-start.3
  15.7 44.7 %all-to-all-start = ((bf16[8,16,1024]{2,0,1:T(8,128)(2,1)}), bf16[8,16,1024]{2,0,1:T(8,128)(2,1)S(1)}, u32[]{:S(2)}, u32[]{:S(2)}) async-start(bf16[8,16,1024]{2,0,1:T(8,128)(2,1)} %bitcast.12), calls=%async_computation | async-start | bytes 524288 | tf_op jit(solution)/shard_map/all_to_all | solution.py:161
  33.1 2.2 %copy-start = (bf16[4,128,4096]{2,1,0:T(8,128)(2,1)S(1)}, bf16[4,128,4096]{2,1,0:T(8,128)(2,1)}, u32[]{:S(2)}) copy-start(bf16[4,128,4096]{2,1,0:T(8,128)(2,1)} %noise_ref.1) | copy-start | bytes 12582916
  46.1 1.3 copy-start.1
  60.4 1.6 %copy-start.2 = (f32[4,1024,128]{2,1,0:T(8,128)S(1)}, f32[4,1024,128]{2,1,0:T(8,128)}, u32[]{:S(2)}) copy-start(f32[4,1024,128]{2,1,0:T(8,128)} %copy-done.1) | copy-start | bytes 6291460
Sparse Core Ops, SparseCore 0:
  15.8 42.2 all-gather.1

commit v3 on v2

--- a/solution.py
+++ b/solution.py
@@ -22,30 +22,109 @@
 ROOT = math.sqrt(M - 1.0)
 inflation = 4.0
 HIGHEST = lax.Precision.HIGHEST
+MESH = pl.DeviceIdType.MESH
 NT = (((1,), (1,)), ((), ()))
 
 
-def prepare(value_ref, spread_ref, local_ref, noise_ref, rhs_ref, weight_ref):
-    def one(k, carry):
+def exchange(ways, value_ref, spread_ref, local_ref, noise_ref, sent_ref, share_ref,
+             got_ref, mine_ref, rhs_ref, weight_ref, send_sem, recv_sem, part_send, part_recv):
+    me = lax.axis_index("st")
+    partner = me + 1 - 2 * lax.rem(me, 2)
+    half = ways // 2
+
+    barrier = pltpu.get_barrier_semaphore()
+
+    def greet(step, carry):
+        peer = lax.rem(me + step, ways)
+        pl.semaphore_signal(barrier, inc=1, device_id={"st": peer}, device_id_type=MESH)
+        return carry
+
+    lax.fori_loop(1, ways, greet, 0)
+    pl.semaphore_wait(barrier, ways - 1)
+
+    def whole(step):
+        peer = lax.rem(me + 2 * step, ways)
+        return pltpu.make_async_remote_copy(
+            src_ref=sent_ref, dst_ref=got_ref.at[me], send_sem=send_sem.at[step],
+            recv_sem=recv_sem.at[me], device_id={"st": peer}, device_id_type=MESH)
+
+    def across(source, slot, src_ref):
+        return pltpu.make_async_remote_copy(
+            src_ref=src_ref, dst_ref=got_ref.at[source], send_sem=send_sem.at[slot],
+            recv_sem=recv_sem.at[source], device_id={"st": partner}, device_id_type=MESH)
+
+    def part(step):
+        peer = lax.rem(me + step, ways)
+        return pltpu.make_async_remote_copy(
+            src_ref=share_ref.at[peer], dst_ref=mine_ref.at[me], send_sem=part_send.at[step],
+            recv_sem=part_recv.at[me], device_id={"st": peer}, device_id_type=MESH)
+
+    def arrived(source):
+        pltpu.make_async_remote_copy(
+            src_ref=sent_ref, dst_ref=got_ref.at[source], send_sem=send_sem.at[0],
+            recv_sem=recv_sem.at[source], device_id={"st": partner}, device_id_type=MESH).wait_recv()
+
+    def loop(low, high, body):
+        lax.fori_loop(low, high, lambda i, c: (body(i), c)[1], 0)
+
+    loop(1, half, lambda step: whole(step).start())
+    across(me, 0, sent_ref).start()
+    loop(1, ways, lambda step: part(step).start())
+    got_ref[me] = sent_ref[...]
+    mine_ref[me] = share_ref[me]
+
+    def one(batch, k):
         cols = pl.ds(pl.multiple_of(k * BLK, BLK), BLK)
-        inv = 1.0 / (math.sqrt(inflation) * spread_ref[0, :, cols])
+        inv = 1.0 / (math.sqrt(inflation) * spread_ref[batch, :, cols])
         var = lax.broadcasted_iota(jnp.int32, (SPAN, BLK), 0) + k * SPAN
-        hit = var == local_ref[0, :, cols]
+        hit = var == local_ref[batch, :, cols]
         placed = jnp.where(hit, inv, 0.0)
         high = placed.astype(jnp.bfloat16)
         low = (placed - high.astype(jnp.float32)).astype(jnp.bfloat16)
-        noise = noise_ref[0, :, cols]
+        noise = noise_ref[batch, :, cols]
         summed = lax.dot_general(high, noise, NT, preferred_element_type=jnp.float32)
         summed += lax.dot_general(low, noise, NT, preferred_element_type=jnp.float32)
         square = placed * inv
         weight = jnp.sum(square, axis=1, keepdims=True)
-        summed += jnp.sum(square * value_ref[0, :, cols], axis=1, keepdims=True)
+        summed += jnp.sum(square * value_ref[batch, :, cols], axis=1, keepdims=True)
         rows = pl.ds(pl.multiple_of(k * SPAN, SPAN), SPAN)
-        rhs_ref[0, rows, :] = summed
-        weight_ref[0, rows, :] = jnp.broadcast_to(weight, (SPAN, M))
-        return carry
-
-    lax.fori_loop(0, NOB, one, 0)
+        rhs_ref[batch, rows, :] = summed
+        weight_ref[batch, rows, :] = jnp.broadcast_to(weight, (SPAN, M))
+
+    def two(i, batch):
+        one(batch, 2 * i)
+        one(batch, 2 * i + 1)
+
+    for batch in range(NB):
+        loop(0, NOB // 2, lambda i: two(i, batch))
+
+    def pass_on(step):
+        source = lax.rem(me + ways - 2 * step, ways)
+        arrived(source)
+        across(source, half + step, got_ref.at[source]).start()
+
+    loop(1, half, pass_on)
+
+    def passed(step):
+        arrived(lax.rem(partner + ways - 2 * step, ways))
+
+    loop(0, half, passed)
+
+    def settle(step):
+        whole(step).wait_send()
+        across(me, half + step, sent_ref).wait_send()
+
+    loop(1, half, settle)
+    across(me, 0, sent_ref).wait_send()
+
+    def parted(step):
+        part(step).wait_send()
+        source = lax.rem(me + ways - step, ways)
+        pltpu.make_async_remote_copy(
+            src_ref=share_ref.at[me], dst_ref=mine_ref.at[source], send_sem=part_send.at[0],
+            recv_sem=part_recv.at[source], device_id={"st": partner}, device_id_type=MESH).wait_recv()
+
+    loop(1, ways, parted)
 
 
 def assimilate(table_ref, owned_ref, mine_ref, rhs_ref, weight_ref, out_ref,
@@ -158,37 +237,52 @@
     ensemble, obs_value, obs_spread, obs_noise, owner, obs_local, loc_count, loc_obs, loc_shift
 ):
     members = ensemble.shape[0]
-    mine = lax.all_to_all(ensemble, "st", split_axis=1, concat_axis=0, tiled=True)
+    ways = M // members
     table = jnp.concatenate([loc_count[:, :, None], loc_obs, loc_shift], axis=2)
-    pad = -(-TABLE // (members * 128)) * 128
-    flat = jnp.pad(table.reshape(TABLE).astype(jnp.bfloat16), (0, members * pad - TABLE))
-    parts = [lax.dynamic_slice_in_dim(ensemble, owner[b] * REGION, REGION, 1) for b in range(NB)]
-    sent = jnp.concatenate(parts + [flat.reshape(members, pad)], axis=1)
-    got = lax.all_gather(sent, "st", axis=0, tiled=True)
-    owned = got[:, :NB * REGION]
-    tables = got[:, NB * REGION:].reshape(-1, members * pad)[:, :TABLE]
+    wide = REGION // 128
+    base = NB * wide * members
+    total = -(-(base + -(-TABLE // 128)) // 16) * 16
+    flat = jnp.pad(table.reshape(TABLE).astype(jnp.bfloat16), (0, (total - base) * 128 - TABLE))
+
+    def tall(x):
+        return x.reshape(members, -1, 128).transpose(1, 0, 2).reshape(-1, 128)
+
+    parts = [tall(lax.dynamic_slice_in_dim(ensemble, owner[b] * REGION, REGION, 1)) for b in range(NB)]
+    sent = jnp.concatenate(parts + [flat.reshape(total - base, 128)], axis=0)
+    share = tall(ensemble).reshape(ways, wide * members, 128)
+    held = -(-wide * members // 16) * 16
+    share = jnp.pad(share, ((0, 0), (0, held - wide * members), (0, 0)))
+
+    vmem = pl.BlockSpec(memory_space=pltpu.VMEM)
+    sums = jax.ShapeDtypeStruct((NB, REGION, M), jnp.float32)
+    got, mine, rhs, weight = pl.pallas_call(
+        functools.partial(exchange, ways),
+        in_specs=[vmem] * 6,
+        out_specs=[vmem] * 4,
+        out_shape=[
+            jax.ShapeDtypeStruct((ways, total, 128), jnp.bfloat16),
+            jax.ShapeDtypeStruct((ways, held, 128), jnp.bfloat16),
+            sums,
+            sums,
+        ],
+        scratch_shapes=[pltpu.SemaphoreType.DMA((ways,))] * 4,
+        compiler_params=pltpu.CompilerParams(
+            collective_id=0, has_side_effects=True, vmem_limit_bytes=40 << 20
+        ),
+        name="exchange",
+    )(obs_value[:, None], obs_spread[:, None], obs_local[:, None], obs_noise, sent, share)
+
+    def across(x, count):
+        return x[:, :count * members].reshape(ways, count, members, 128).transpose(0, 2, 1, 3).reshape(M, count * 128)
+
+    owned = across(got, NB * wide)
+    mine = across(mine, wide)
+    tables = got[:, base:].reshape(ways, -1)[:, :TABLE]
     picked = [lax.dynamic_slice_in_dim(tables, owner[b], 1, 0).reshape(TABLE) for b in range(NB)]
     all_tables = jnp.concatenate(
         [jnp.concatenate(picked).astype(jnp.int32), table.reshape(TABLE)]
     )
 
-    rhs, weight = pl.pallas_call(
-        prepare,
-        grid=(NB,),
-        in_specs=[
-            pl.BlockSpec((1, 1, NOB * BLK), lambda b: (b, 0, 0)),
-            pl.BlockSpec((1, 1, NOB * BLK), lambda b: (b, 0, 0)),
-            pl.BlockSpec((1, 1, NOB * BLK), lambda b: (b, 0, 0)),
-            pl.BlockSpec((1, M, NOB * BLK), lambda b: (b, 0, 0)),
-        ],
-        out_specs=[pl.BlockSpec((1, REGION, M), lambda b: (b, 0, 0))] * 2,
-        out_shape=[jax.ShapeDtypeStruct((NB, REGION, M), jnp.float32)] * 2,
-        compiler_params=pltpu.CompilerParams(vmem_limit_bytes=16 << 20),
-        cost_estimate=pl.CostEstimate(flops=1 << 29, bytes_accessed=8 << 20, transcendentals=0),
-        name="prepare",
-    )(obs_value[:, None], obs_spread[:, None], obs_local[:, None], obs_noise)
-
-    vmem = pl.BlockSpec(memory_space=pltpu.VMEM)
     return pl.pallas_call(
         assimilate,
         in_specs=[pl.BlockSpec(memory_space=pltpu.SMEM)] + [vmem] * 4,

time: 142 us -> 124 us (0.87)
  the two profiles are of different devices: /device:TPU:0 before, /device:TPU:14 now
where the time goes in v3:
time: 124 us; the launch traced here: 122 us
  Pallas kernels  97 us (78%)
  local copies, waits for them, and re-layouts  14.5 us (12%)
  between operations  9.7 us (8%)
    pallas_call x1, Pallas kernels, shards(): pl.pallas_call(assimilate, in_specs=[pl.BlockSpec(memory_space=pltpu.SMEM...  74 us
    pallas_call x1, Pallas kernels, shards(): pl.pallas_call(functools.partial(exchange, ways), in_specs=[vmem] * 6, ou...  23 us
    unnamed x17, local copies, waits for them, and re-layouts  9.38 us

profile of v3, /device:TPU:14, one launch (start us, length us, event | category | flops | bytes accessed | tf_op | source)
XLA Modules:
  0.0 122.2 jit_solution(6872689552926952673)
XLA Ops:
  0.0 0.8 copy.10
  0.8 0.8 pad_add_fusion
  1.6 0.1 reshape.69
  1.7 0.9 broadcast_in_dim.12.value_ref
  2.6 0.9 broadcast_in_dim.13.spread_ref
  3.5 0.9 broadcast_in_dim.14.local_ref
  4.3 1.4 %fusion.4 = (s32[1]{0:T(128)}, s32[1]{0:T(128)}, s32[1]{0:T(128)}, s32[1]{0:T(128)}) fusion(s32[4]{0:T(128)} %param.13), kind=kLoop, calls=%fused_computation.18 | loop fusion | bytes 32 | tf_op jit(solution)/shard_map/slice | solution.py:250
  6.4 0.7 bitcast_dynamic-update-slice_fusion.3
  7.7 0.7 bitcast_dynamic-update-slice_fusion.2
  9.0 0.7 bitcast_dynamic-update-slice_fusion.1
  10.4 0.7 bitcast_dynamic-update-slice_fusion
  11.1 0.0 copy-start
  11.1 2.2 %copy-done = bf16[4,128,4096]{2,1,0:T(8,128)(2,1)S(1)} copy-done((bf16[4,128,4096]{2,1,0:T(8,128)(2,1)S(1)}, bf16[4,128,4096]{2,1,0:T(8,128)(2,1)}, u32[]{:S(2)}) %copy-start) | copy-done | bytes 4194328
  13.3 0.0 copy-start.3
  13.3 0.9 copy-done.3
  14.3 23.0 %exchange.1 = (bf16[16,272,128]{2,1,0:T(8,128)(2,1)S(1)}, bf16[16,64,128]{2,1,0:T(8,128)(2,1)S(1)}, f32[4,1024,128]{2,1,0:T(8,128)S(1)}, f32[4,1024,128]{2,1,0:T(8,128)S(1)}) custom-call(f32[4,1,4096]{2,1,0:T(1,128)S(1)} %broadcast_in_dim.12.value_ref, f32[4,1,4096]{2,1,0:T(1,128)S(1)} %broadcast_in_dim.13.spread_ref, ...), custom_call_target="tpu_custom_call" | custom-call | tf_op jit(solution)/shard_map/exchange/pallas_call | solution.py:258
  37.3 0.0 copy-start.1
  37.3 1.3 %copy-done.1 = f32[4,1024,128]{2,1,0:T(8,128)} copy-done((f32[4,1024,128]{2,1,0:T(8,128)}, f32[4,1024,128]{2,1,0:T(8,128)S(1)}, u32[]{:S(2)}) %copy-start.1) | copy-done | bytes 2097176
  38.6 0.0 copy-start.4
  38.7 0.7 copy-done.4
  39.4 0.0 copy-start.5
  46.6 0.0 copy-start.2
  46.6 0.1 maximum_convert_fusion
  46.7 0.1 pad_add_fusion.1.table_ref
  46.8 0.1 slice_bitcast_fusion.owned_ref
  46.9 0.0 copy-done.5
  46.9 1.3 %copy-done.2 = f32[4,1024,128]{2,1,0:T(8,128)S(1)} copy-done((f32[4,1024,128]{2,1,0:T(8,128)S(1)}, f32[4,1024,128]{2,1,0:T(8,128)}, u32[]{:S(2)}) %copy-start.2) | copy-done | bytes 2097176
  48.2 74.0 %assimilate.1 = bf16[128,1024]{1,0:T(8,128)(2,1)} custom-call(s32[720]{0:T(1024)S(1)} %pad_add_fusion.1.table_ref, bf16[128,4096]{1,0:T(8,128)(2,1)S(1)} %slice_bitcast_fusion.owned_ref, bf16[128,1024]{1,0:T(8,128)(2,1)S(1)} %bitcast.52, f32[4,1024,128]{2,1,0:T(8,128)S(1)} %get-tuple-element.11.rhs_ref, f32[4,1024,128]{2,1,0:T(8,128)S(1)} %copy-done.2), custom_call_target="tpu_custom_call" | custom-call | tf_op jit(solution)/shard_map/assimilate/pallas_call | solution.py:286
  (6 shorter events, 0.1 us)
Async XLA Ops:
  11.1 2.2 %copy-start = (bf16[4,128,4096]{2,1,0:T(8,128)(2,1)S(1)}, bf16[4,128,4096]{2,1,0:T(8,128)(2,1)}, u32[]{:S(2)}) copy-start(bf16[4,128,4096]{2,1,0:T(8,128)(2,1)} %noise_ref.1) | copy-start | bytes 12582916
  13.3 0.9 copy-start.3
  37.3 1.4 %copy-start.1 = (f32[4,1024,128]{2,1,0:T(8,128)}, f32[4,1024,128]{2,1,0:T(8,128)S(1)}, u32[]{:S(2)}) copy-start(f32[4,1024,128]{2,1,0:T(8,128)S(1)} %get-tuple-element.12.weight_ref) | copy-start | bytes 6291460
  38.6 0.7 copy-start.4
  39.4 7.6 %copy-start.5 = (bf16[16,64,128]{2,1,0:T(8,128)(2,1)S(1)}, bf16[16,64,128]{2,1,0:T(8,128)(2,1)}, u32[]{:S(2)}) copy-start(bf16[16,64,128]{2,1,0:T(8,128)(2,1)} %copy-done.4) | copy-start | bytes 786436
  46.6 1.6 %copy-start.2 = (f32[4,1024,128]{2,1,0:T(8,128)S(1)}, f32[4,1024,128]{2,1,0:T(8,128)}, u32[]{:S(2)}) copy-start(f32[4,1024,128]{2,1,0:T(8,128)} %copy-done.1) | copy-start | bytes 6291460

commit v4 on v3

--- a/solution.py
+++ b/solution.py
@@ -21,9 +21,21 @@
 TABLE = NB * BLOCKS * ENTRY
 ROOT = math.sqrt(M - 1.0)
 inflation = 4.0
-HIGHEST = lax.Precision.HIGHEST
+NN = (((1,), (0,)), ((), ()))
 MESH = pl.DeviceIdType.MESH
 NT = (((1,), (1,)), ((), ()))
+
+
+def split(x):
+    high = x.astype(jnp.bfloat16)
+    return high, (x - high.astype(jnp.float32)).astype(jnp.bfloat16)
+
+
+def dot3(x, y, dims):
+    def one(a, b):
+        return lax.dot_general(a, b, dims, preferred_element_type=jnp.float32)
+
+    return one(x[0], y[0]) + (one(x[0], y[1]) + one(x[1], y[0]))
 
 
 def exchange(ways, value_ref, spread_ref, local_ref, noise_ref, sent_ref, share_ref,
@@ -163,14 +175,15 @@
             scaled = anom * (weight * inverse * (1.0 / ROOT))
             factor[rows, :] = scaled
             right[rows, :] = (rhs_ref[batch, rows, :] - weight * x) * (inverse * (1.0 / ROOT))
-            gram = lax.dot_general(scaled, scaled, NT, precision=HIGHEST, preferred_element_type=jnp.float32)
+            pieces = split(scaled)
+            gram = dot3(pieces, pieces, NT)
             row = lax.broadcasted_iota(jnp.int32, (SPAN, PAIR), 0)
             eye = jnp.where(row == jnp.where(first, lane, lane - SPAN), 1.0, 0.0)
             packed = jnp.where(first, gram[:SPAN], gram[SPAN:]) + eye
             system[pl.ds(pl.multiple_of(p * SPAN, SPAN), SPAN), :] = packed
             return carry
 
-        lax.fori_loop(0, NOB // 2, build, 0, unroll=4)
+        lax.fori_loop(0, NOB // 2, build, 0, unroll=8)
 
         def eliminate(j, carry):
             pick = jnp.where(first, j, j + SPAN)
@@ -195,35 +208,44 @@
             rows = pl.ds(pl.multiple_of(p * PAIR, PAIR), PAIR)
             packed = system[pl.ds(pl.multiple_of(p * SPAN, SPAN), SPAN), :]
             whole = jnp.concatenate([jnp.where(first, packed, 0.0), jnp.where(first, 0.0, packed)], axis=0)
-            solved = jnp.dot(whole, right[rows, :], precision=HIGHEST, preferred_element_type=jnp.float32)
+            solved = split(dot3(split(whole), split(right[rows, :]), NN))
             left = factor[rows, :].T
             lanes = lax.broadcasted_iota(jnp.int32, (M, PAIR), 1) < SPAN
             for half, keep in enumerate((lanes, jnp.logical_not(lanes))):
-                made = jnp.dot(jnp.where(keep, left, 0.0), solved, precision=HIGHEST, preferred_element_type=jnp.float32)
+                made = dot3(split(jnp.where(keep, left, 0.0)), solved, NN)
                 weights[2 * p + half] = made.astype(jnp.bfloat16)
             return carry
 
-        lax.fori_loop(0, NOB // 2, finish, 0, unroll=4)
+        lax.fori_loop(0, NOB // 2, finish, 0, unroll=8)
 
         def update(index, carry):
-            region = batch + 1 + index // BLOCKS
-            block = index % BLOCKS
-            base = ((region * NB + batch) * BLOCKS + block) * ENTRY
-            rows = pl.ds(pl.multiple_of((batch + 1) * REGION + index * BLK, BLK), BLK)
-            x = state[rows, :]
-            anoms[...] = (x - jnp.mean(x, axis=1, keepdims=True)).astype(jnp.bfloat16)
-
-            def slot(j, carry):
-                k = table_ref[base + 1 + j]
-                shift = table_ref[base + 1 + KMAX + j]
-                term = jnp.dot(anoms[...], weights[k], preferred_element_type=jnp.float32)
-                state[rows, :] += term * taper[pl.ds(BLK - shift, BLK), :]
-                return carry
-
-            lax.fori_loop(0, table_ref[base], slot, 0)
+            region = batch + 1 + index
+            blocks = range(BLOCKS)
+            bases = [((region * NB + batch) * BLOCKS + i) * ENTRY for i in blocks]
+            rows = [pl.ds(pl.multiple_of(region * REGION + i * BLK, BLK), BLK) for i in blocks]
+
+            def term(i, j, anom):
+                k = table_ref[bases[i] + 1 + j]
+                shift = table_ref[bases[i] + 1 + KMAX + j]
+                made = jnp.dot(anom, weights[k], preferred_element_type=jnp.float32)
+                return made * taper[pl.ds(BLK - shift, BLK), :]
+
+            for i in blocks:
+                x = state[rows[i], :]
+                anom = (x - jnp.mean(x, axis=1, keepdims=True)).astype(jnp.bfloat16)
+                anoms[i] = anom
+                state[rows[i], :] = x + term(i, 0, anom)
+
+            for i in blocks:
+
+                def slot(j, carry):
+                    state[rows[i], :] += term(i, j, anoms[i])
+                    return carry
+
+                lax.fori_loop(1, table_ref[bases[i]], slot, 0)
             return carry
 
-        lax.fori_loop(0, (NB - batch) * BLOCKS, update, 0)
+        lax.fori_loop(0, NB - batch, update, 0)
 
     def leave(c, carry):
         at = pl.multiple_of(c * 128, 128)
@@ -295,7 +317,7 @@
             pltpu.VMEM((REGION, M), jnp.float32),
             pltpu.VMEM((REGION, M), jnp.float32),
             pltpu.VMEM((NOB, M, M), jnp.bfloat16),
-            pltpu.VMEM((BLK, M), jnp.bfloat16),
+            pltpu.VMEM((BLOCKS, BLK, M), jnp.bfloat16),
         ],
         compiler_params=pltpu.CompilerParams(vmem_limit_bytes=40 << 20),
         name="assimilate",

time: 124 us -> 109 us (0.88); the launches traced: 122 us -> 109 us
  Pallas kernels: 97 us -> 83.8 us
    pallas_call x1, Pallas kernels: 74 us -> 60.8 us  [shards(): pl.pallas_call(assimilate, in_specs=[pl.BlockSpec(memory_space=pltpu.SMEM...]
where the time goes in v4:
time: 109 us
  Pallas kernels  83.8 us (77%)
  local copies, waits for them, and re-layouts  14.5 us (13%)
  between operations  9.7 us (9%)
    pallas_call x1, Pallas kernels, shards(): pl.pallas_call(assimilate, in_specs=[pl.BlockSpec(memory_space=pltpu.SMEM...  60.8 us
    pallas_call x1, Pallas kernels, shards(): pl.pallas_call(functools.partial(exchange, ways), in_specs=[vmem] * 6, ou...  23 us
    unnamed x17, local copies, waits for them, and re-layouts  9.38 us

profile of v4, /device:TPU:14, one launch (start us, length us, event | category | flops | bytes accessed | tf_op | source)
XLA Modules:
  0.0 109.0 jit_solution(5386903469352592016)
XLA Ops:
  0.0 0.8 copy.10
  0.8 0.8 pad_add_fusion
  1.6 0.1 reshape.69
  1.7 0.9 broadcast_in_dim.12.value_ref
  2.6 0.9 broadcast_in_dim.13.spread_ref
  3.5 0.9 broadcast_in_dim.14.local_ref
  4.3 1.4 %fusion.4 = (s32[1]{0:T(128)}, s32[1]{0:T(128)}, s32[1]{0:T(128)}, s32[1]{0:T(128)}) fusion(s32[4]{0:T(128)} %param.13), kind=kLoop, calls=%fused_computation.18 | loop fusion | bytes 32 | tf_op jit(solution)/shard_map/slice | solution.py:272
  6.4 0.7 bitcast_dynamic-update-slice_fusion.3
  7.7 0.7 bitcast_dynamic-update-slice_fusion.2
  9.0 0.7 bitcast_dynamic-update-slice_fusion.1
  10.4 0.7 bitcast_dynamic-update-slice_fusion
  11.1 0.0 copy-start
  11.1 2.2 %copy-done = bf16[4,128,4096]{2,1,0:T(8,128)(2,1)S(1)} copy-done((bf16[4,128,4096]{2,1,0:T(8,128)(2,1)S(1)}, bf16[4,128,4096]{2,1,0:T(8,128)(2,1)}, u32[]{:S(2)}) %copy-start) | copy-done | bytes 4194328
  13.3 0.0 copy-start.3
  13.3 0.9 copy-done.3
  14.3 23.0 %exchange.1 = (bf16[16,272,128]{2,1,0:T(8,128)(2,1)S(1)}, bf16[16,64,128]{2,1,0:T(8,128)(2,1)S(1)}, f32[4,1024,128]{2,1,0:T(8,128)S(1)}, f32[4,1024,128]{2,1,0:T(8,128)S(1)}) custom-call(f32[4,1,4096]{2,1,0:T(1,128)S(1)} %broadcast_in_dim.12.value_ref, f32[4,1,4096]{2,1,0:T(1,128)S(1)} %broadcast_in_dim.13.spread_ref, ...), custom_call_target="tpu_custom_call" | custom-call | tf_op jit(solution)/shard_map/exchange/pallas_call | solution.py:280
  37.3 0.0 copy-start.1
  37.3 1.3 %copy-done.1 = f32[4,1024,128]{2,1,0:T(8,128)} copy-done((f32[4,1024,128]{2,1,0:T(8,128)}, f32[4,1024,128]{2,1,0:T(8,128)S(1)}, u32[]{:S(2)}) %copy-start.1) | copy-done | bytes 2097176
  38.6 0.0 copy-start.4
  38.7 0.7 copy-done.4
  39.4 0.0 copy-start.5
  46.6 0.0 copy-start.2
  46.6 0.1 maximum_convert_fusion
  46.7 0.1 pad_add_fusion.1.table_ref
  46.8 0.1 slice_bitcast_fusion.owned_ref
  46.9 0.0 copy-done.5
  46.9 1.3 %copy-done.2 = f32[4,1024,128]{2,1,0:T(8,128)S(1)} copy-done((f32[4,1024,128]{2,1,0:T(8,128)S(1)}, f32[4,1024,128]{2,1,0:T(8,128)}, u32[]{:S(2)}) %copy-start.2) | copy-done | bytes 2097176
  48.2 60.8 %assimilate.1 = bf16[128,1024]{1,0:T(8,128)(2,1)} custom-call(s32[720]{0:T(1024)S(1)} %pad_add_fusion.1.table_ref, bf16[128,4096]{1,0:T(8,128)(2,1)S(1)} %slice_bitcast_fusion.owned_ref, bf16[128,1024]{1,0:T(8,128)(2,1)S(1)} %bitcast.52, f32[4,1024,128]{2,1,0:T(8,128)S(1)} %get-tuple-element.11.rhs_ref, f32[4,1024,128]{2,1,0:T(8,128)S(1)} %copy-done.2), custom_call_target="tpu_custom_call" | custom-call | tf_op jit(solution)/shard_map/assimilate/pallas_call | solution.py:308
  (6 shorter events, 0.1 us)
Async XLA Ops:
  11.1 2.2 %copy-start = (bf16[4,128,4096]{2,1,0:T(8,128)(2,1)S(1)}, bf16[4,128,4096]{2,1,0:T(8,128)(2,1)}, u32[]{:S(2)}) copy-start(bf16[4,128,4096]{2,1,0:T(8,128)(2,1)} %noise_ref.1) | copy-start | bytes 12582916
  13.3 0.9 copy-start.3
  37.3 1.4 %copy-start.1 = (f32[4,1024,128]{2,1,0:T(8,128)}, f32[4,1024,128]{2,1,0:T(8,128)S(1)}, u32[]{:S(2)}) copy-start(f32[4,1024,128]{2,1,0:T(8,128)S(1)} %get-tuple-element.12.weight_ref) | copy-start | bytes 6291460
  38.6 0.7 copy-start.4
  39.4 7.6 %copy-start.5 = (bf16[16,64,128]{2,1,0:T(8,128)(2,1)S(1)}, bf16[16,64,128]{2,1,0:T(8,128)(2,1)}, u32[]{:S(2)}) copy-start(bf16[16,64,128]{2,1,0:T(8,128)(2,1)} %copy-done.4) | copy-start | bytes 786436
  46.6 1.6 %copy-start.2 = (f32[4,1024,128]{2,1,0:T(8,128)S(1)}, f32[4,1024,128]{2,1,0:T(8,128)}, u32[]{:S(2)}) copy-start(f32[4,1024,128]{2,1,0:T(8,128)} %copy-done.1) | copy-start | bytes 6291460

commit v5 on v4

--- a/solution.py
+++ b/solution.py
@@ -139,7 +139,14 @@
     loop(1, ways, parted)
 
 
-def assimilate(table_ref, owned_ref, mine_ref, rhs_ref, weight_ref, out_ref,
+def pack(owner_ref, share_ref, flat_ref, sent_ref):
+    rows = (sent_ref.shape[0] - flat_ref.shape[0]) // NB
+    for b in range(NB):
+        sent_ref[b * rows:(b + 1) * rows, :] = share_ref[owner_ref[b]][:rows]
+    sent_ref[NB * rows:, :] = flat_ref[...]
+
+
+def assimilate(ways, owner_ref, table_ref, owned_ref, mine_ref, rhs_ref, weight_ref, out_ref,
                state, taper, system, right, factor, weights, anoms):
     lane = lax.broadcasted_iota(jnp.int32, (SPAN, PAIR), 1)
     first = lane < SPAN
@@ -221,7 +228,8 @@
         def update(index, carry):
             region = batch + 1 + index
             blocks = range(BLOCKS)
-            bases = [((region * NB + batch) * BLOCKS + i) * ENTRY for i in blocks]
+            place = jnp.where(region == NB, ways, owner_ref[jnp.minimum(region, NB - 1)])
+            bases = [place * TABLE + (batch * BLOCKS + i) * ENTRY for i in blocks]
             rows = [pl.ds(pl.multiple_of(region * REGION + i * BLK, BLK), BLK) for i in blocks]
 
             def term(i, j, anom):
@@ -269,13 +277,20 @@
     def tall(x):
         return x.reshape(members, -1, 128).transpose(1, 0, 2).reshape(-1, 128)
 
-    parts = [tall(lax.dynamic_slice_in_dim(ensemble, owner[b] * REGION, REGION, 1)) for b in range(NB)]
-    sent = jnp.concatenate(parts + [flat.reshape(total - base, 128)], axis=0)
     share = tall(ensemble).reshape(ways, wide * members, 128)
     held = -(-wide * members // 16) * 16
     share = jnp.pad(share, ((0, 0), (0, held - wide * members), (0, 0)))
 
     vmem = pl.BlockSpec(memory_space=pltpu.VMEM)
+    smem = pl.BlockSpec(memory_space=pltpu.SMEM)
+    sent = pl.pallas_call(
+        pack,
+        in_specs=[smem, vmem, vmem],
+        out_specs=vmem,
+        out_shape=jax.ShapeDtypeStruct((total, 128), jnp.bfloat16),
+        compiler_params=pltpu.CompilerParams(vmem_limit_bytes=16 << 20),
+        name="pack",
+    )(owner, share, flat.reshape(total - base, 128))
     sums = jax.ShapeDtypeStruct((NB, REGION, M), jnp.float32)
     got, mine, rhs, weight = pl.pallas_call(
         functools.partial(exchange, ways),
@@ -300,14 +315,11 @@
     owned = across(got, NB * wide)
     mine = across(mine, wide)
     tables = got[:, base:].reshape(ways, -1)[:, :TABLE]
-    picked = [lax.dynamic_slice_in_dim(tables, owner[b], 1, 0).reshape(TABLE) for b in range(NB)]
-    all_tables = jnp.concatenate(
-        [jnp.concatenate(picked).astype(jnp.int32), table.reshape(TABLE)]
-    )
+    all_tables = jnp.concatenate([tables.astype(jnp.int32).reshape(-1), table.reshape(TABLE)])
 
     return pl.pallas_call(
-        assimilate,
-        in_specs=[pl.BlockSpec(memory_space=pltpu.SMEM)] + [vmem] * 4,
+        functools.partial(assimilate, ways),
+        in_specs=[smem, smem] + [vmem] * 4,
         out_specs=vmem,
         out_shape=jax.ShapeDtypeStruct((M, REGION), jnp.bfloat16),
         scratch_shapes=[
@@ -321,7 +333,7 @@
         ],
         compiler_params=pltpu.CompilerParams(vmem_limit_bytes=40 << 20),
         name="assimilate",
-    )(all_tables, owned, mine, rhs, weight)
+    )(owner, all_tables, owned, mine, rhs, weight)
 
 
 def solution(mesh):

time: 109 us -> 98 us (0.90)
  between operations: 9.7 us -> 0.11 us
  local copies, waits for them, and re-layouts: 14.5 us -> 11.3 us
  Pallas kernels: 83.8 us -> 85.5 us
    unnamed x17 -> x15, local copies, waits for them, and re-layouts: 9.38 us -> 7.56 us
    pallas_call x1 -> x2, Pallas kernels: 60.8 us -> 62.5 us  [the longest x1 61.9 us: shards(): pl.pallas_call(functools.partial(assimilate, ways), in_specs=[smem, smem]...]
    slice x1 -> x0, local copies, waits for them, and re-layouts: 1.42 us -> none  [shards(): owner[b] * REGION]
where the time goes in v5:
time: 98 us; the launch traced here: 97.7 us
  Pallas kernels  85.5 us (87%)
  local copies, waits for them, and re-layouts  11.3 us (12%)
    pallas_call x1, Pallas kernels, shards(): pl.pallas_call(functools.partial(assimilate, ways), in_specs=[smem, smem]...  61.9 us
    pallas_call x1, Pallas kernels, shards(): pl.pallas_call(functools.partial(exchange, ways), in_specs=[vmem] * 6, ou...  23 us
    unnamed x15, local copies, waits for them, and re-layouts  7.56 us

profile of v5, /device:TPU:14, one launch (start us, length us, event | category | flops | bytes accessed | tf_op | source)
XLA Modules:
  0.0 97.7 jit_solution(2913460342590090364)
XLA Ops:
  0.0 0.8 copy.10
  0.8 0.8 pad_add_fusion.1
  1.6 0.1 reshape.32
  1.7 0.0 copy-start.3
  1.7 0.9 copy-done.3
  2.7 0.0 copy-start.5
  2.7 0.7 copy-done.5
  3.3 0.5 pack.1.sent_ref
  3.9 0.9 broadcast_in_dim.12.value_ref
  4.8 0.9 broadcast_in_dim.13.spread_ref
  5.6 0.9 broadcast_in_dim.14.local_ref
  6.5 0.0 copy-start
  6.5 2.2 %copy-done = bf16[4,128,4096]{2,1,0:T(8,128)(2,1)S(1)} copy-done((bf16[4,128,4096]{2,1,0:T(8,128)(2,1)S(1)}, bf16[4,128,4096]{2,1,0:T(8,128)(2,1)}, u32[]{:S(2)}) %copy-start) | copy-done | bytes 4194328
  8.7 0.0 copy-start.4
  8.7 0.9 copy-done.4
  9.7 23.0 %exchange.1 = (bf16[16,272,128]{2,1,0:T(8,128)(2,1)S(1)}, bf16[16,64,128]{2,1,0:T(8,128)(2,1)S(1)}, f32[4,1024,128]{2,1,0:T(8,128)S(1)}, f32[4,1024,128]{2,1,0:T(8,128)S(1)}) custom-call(f32[4,1,4096]{2,1,0:T(1,128)S(1)} %broadcast_in_dim.12.value_ref, f32[4,1,4096]{2,1,0:T(1,128)S(1)} %broadcast_in_dim.13.spread_ref, ...), custom_call_target="tpu_custom_call" | custom-call | tf_op jit(solution)/shard_map/exchange/pallas_call | solution.py:295
  32.7 0.0 copy-start.1
  32.7 1.3 %copy-done.1 = f32[4,1024,128]{2,1,0:T(8,128)} copy-done((f32[4,1024,128]{2,1,0:T(8,128)}, f32[4,1024,128]{2,1,0:T(8,128)S(1)}, u32[]{:S(2)}) %copy-start.1) | copy-done | bytes 2097176
  34.1 0.0 copy-start.6
  34.1 0.1 reshape.42
  34.2 0.0 copy-start.2
  34.2 0.1 slice_bitcast_fusion.owned_ref
  34.3 0.4 copy-done.6
  34.7 1.1 %copy-done.2 = f32[4,1024,128]{2,1,0:T(8,128)S(1)} copy-done((f32[4,1024,128]{2,1,0:T(8,128)S(1)}, f32[4,1024,128]{2,1,0:T(8,128)}, u32[]{:S(2)}) %copy-start.2) | copy-done | bytes 2097176
  35.8 61.9 %assimilate.1 = bf16[128,1024]{1,0:T(8,128)(2,1)} custom-call(s32[4]{0:T(128)S(1)} %copy-done.6, s32[2448]{0:T(1024)S(1)} %pad_add_fusion.table_ref, bf16[128,4096]{1,0:T(8,128)(2,1)S(1)} %slice_bitcast_fusion.owned_ref, bf16[128,1024]{1,0:T(8,128)(2,1)S(1)} %bitcast.25, f32[4,1024,128]{2,1,0:T(8,128)S(1)} %get-tuple-element.11.rhs_ref, ...), custom_call_target="tpu_custom_call" | custom-call | tf_op jit(solution)/shard_map/assimilate/pallas_call | solution.py:320
  (6 shorter events, 0.1 us)
Async XLA Ops:
  1.7 1.0 copy-start.3
  2.7 0.7 copy-start.5
  6.5 2.2 %copy-start = (bf16[4,128,4096]{2,1,0:T(8,128)(2,1)S(1)}, bf16[4,128,4096]{2,1,0:T(8,128)(2,1)}, u32[]{:S(2)}) copy-start(bf16[4,128,4096]{2,1,0:T(8,128)(2,1)} %noise_ref.1) | copy-start | bytes 12582916
  8.7 0.9 copy-start.4
  32.7 1.3 %copy-start.1 = (f32[4,1024,128]{2,1,0:T(8,128)}, f32[4,1024,128]{2,1,0:T(8,128)S(1)}, u32[]{:S(2)}) copy-start(f32[4,1024,128]{2,1,0:T(8,128)S(1)} %get-tuple-element.12.weight_ref) | copy-start | bytes 6291460
  34.1 0.7 copy-start.6
  34.2 1.6 %copy-start.2 = (f32[4,1024,128]{2,1,0:T(8,128)S(1)}, f32[4,1024,128]{2,1,0:T(8,128)}, u32[]{:S(2)}) copy-start(f32[4,1024,128]{2,1,0:T(8,128)} %copy-done.1) | copy-start | bytes 6291460
